TPU v7x, 32 devices: a whole 2x2x4 slice. The times are simulated.
32 devices in a mesh: group: 2 (over x), term: 16 (over z, y, core).
Axes of the slice: x: 2, y: 2, z: 4, core: 2. Of those that a mesh axis runs over, the one named last changes fastest.
Arguments:
- vectors: bfloat16 [6, 2048, 256], P('group', 'term'), parts along dimension 0, may hold values from -6 to 6
- left_ops: bfloat16 [1024, 256, 256], P(('group', 'term')), parts along dimension 0, may hold values from -8 to 8
- right_ops: bfloat16 [1024, 256, 256], P(('group', 'term')), parts along dimension 0, may hold values from -8 to 8
- coefficient: float32 [1024], P(('group', 'term')), parts along dimension 0, may hold values from 0.5 to 2
- source: int32 [1024], P(('group', 'term')), parts along dimension 0, may hold values from 0 to 7
- target: int32 [1024], P(('group', 'term')), parts along dimension 0, may hold values from 0 to 7
Outputs:
- sigma: float32 [6, 2048, 256], P('group', 'term'), parts along dimension 0
- residual: float32 [6, 2048, 256], P('group', 'term'), parts along dimension 0
- subspace: float32 [6, 3], P('group'), parts along dimension 0
There are 2 independent parts, one for each index of `group`. A program takes and returns all parts, laid end to end along the dimension named above; each array names one. Nothing has to cross between parts.
All inputs are finite; a program needn't handle non-finite values.
Results may differ from a plain program's by a relative error of at most 0.0015.
Values may be sent and summed in bfloat16 or wider, within the bound.
A program may use at most 128 MiB of HBM per device.

v0:
```python
import jax
import jax.numpy as jnp
from jax import lax
from jax.sharding import PartitionSpec as P


def local(vectors, left_ops, right_ops, coefficient, source, target):
    nvec, rows_dev, width = vectors.shape
    terms_dev = left_ops.shape[0]
    devices = lax.axis_size("term")
    sectors = rows_dev * devices // width
    factor = sectors / (terms_dev * devices)
    whole = lax.all_gather(vectors, "term", axis=1, tiled=True)
    blocks = whole.reshape(nvec, sectors, width, width)
    picked = jnp.take(blocks, source, axis=1)
    inner = jnp.einsum(
        "tab,vtbc->vtac", left_ops, picked, preferred_element_type=jnp.float32
    ).astype(jnp.bfloat16)
    outer = jnp.einsum("vtac,tdc->vtad", inner, right_ops, preferred_element_type=jnp.float32)
    outer = outer * (coefficient * factor)[None, :, None, None]
    sector_ids = jnp.arange(sectors, dtype=jnp.int32)
    onehot = (target[:, None] == sector_ids[None, :]).astype(jnp.float32)
    partial_value = jnp.einsum("vtad,ts->vsad", outer, onehot, precision=lax.Precision.HIGHEST)
    partial_value = partial_value.reshape(nvec, sectors * width, width)
    own = vectors.astype(jnp.float32)
    sigma = lax.psum_scatter(partial_value, "term", scatter_dimension=1, tiled=True)
    local_proj = jnp.einsum("vrb,wrb->vw", own, sigma, precision=lax.Precision.HIGHEST)
    local_norm = jnp.sum(own * own, axis=(1, 2))
    proj, norm2 = lax.psum((local_proj, local_norm), "term")
    theta = jnp.diagonal(proj) / norm2
    residual = sigma - theta[:, None, None] * own
    subspace = proj / jnp.sqrt(norm2[:, None] * norm2[None, :])
    return (sigma, residual, subspace)


def solution(mesh):
    in_specs = (
        P("group", "term", None),
        P(("group", "term"), None, None),
        P(("group", "term"), None, None),
        P(("group", "term")),
        P(("group", "term")),
        P(("group", "term")),
    )
    out_specs = (P("group", "term", None), P("group", "term", None), P("group", None))
    return jax.shard_map(local, mesh=mesh, in_specs=in_specs, out_specs=out_specs, check_vma=False)
```

profile of v0, /device:TPU:0, one launch (start us, length us, event | category | flops | bytes accessed | tf_op | source)
XLA Modules:
  0.0 245.2 jit_solution(12536813234886539150)
XLA Ops:
  7.2 0.0 all-gather.2.cloned.1.call-start
  7.2 0.7 all-gather.2.cloned.1.call-update
  7.9 0.0 reduce-scatter.2.cloned.1.call-start
  7.9 0.7 compare_select_fusion
  8.6 0.7 compare_and_fusion
  9.3 0.7 broadcast_multiply_fusion
  9.9 48.2 %all-gather.2.cloned.1.call-done = bf16[3,2048,256]{2,1,0:T(8,128)(2,1)} async-done(((bf16[3,128,256]{2,1,0:T(8,128)(2,1)}), bf16[3,2048,256]{2,1,0:T(8,128)(2,1)}) %all-gather.2.cloned.1.call-update) | async-done | bytes 3145744 | tf_op jit(solution)/shard_map/all_gather | solution.py:13
  58.1 8.6 %gather_fusion = bf16[32,3,256,256]{3,2,1,0:T(8,128)(2,1)} fusion(bf16[3,8,256,256]{3,2,1,0:T(8,128)(2,1)} %bitcast.43, s32[1024]{0:T(1024)S(1)} %pad_clamp_fusion), kind=kCustom, calls=%fused_computation | custom fusion | bytes 25165952 | tf_op jit(solution)/shard_map/jit(_take)/gather | solution.py:15
  66.7 0.0 copy-start.1
  66.7 17.6 %fusion.2 = f32[32,3,256,256]{3,2,1,0:T(8,128)} fusion(bf16[32,3,256,256]{3,2,1,0:T(8,128)(2,1)} %gather_fusion, pred[32]{0:T(512)(128)(4,1)S(1)} %compare_and_fusion, bf16[32,256,256]{2,1,0:T(8,128)(2,1)} %param.8, bf16[32,256,256]{2,1,0:T(8,128)(2,1)} %param.7), kind=kOutput, calls=%fused_computation.5 | convolution fusion | flops 6455033856 | bytes 46137376 | tf_op jit(solution)/shard_map/vtac,tdc->vtad/dot_general | solution.py:19
  84.4 0.0 copy-done.1
  84.4 28.3 %fusion.19 = f32[3,8,256,256]{3,1,2,0:T(8,128)S(1)} fusion(f32[32,3,256,256]{3,2,1,0:T(8,128)} %fusion.2, f32[32]{0:T(128)S(1)} %broadcast_multiply_fusion, s32[32]{0:T(128)S(1)} %copy-done.1), kind=kOutput, calls=%fused_computation.16 | convolution fusion | flops 610271488 | bytes 31457536 | tf_op jit(solution)/shard_map/vtad,ts->vsad/dot_general | solution.py:23
  112.7 0.0 copy-start
  112.7 4.5 %copy.12 = f32[3,8,256,256]{3,2,1,0:T(8,128)} copy(f32[3,8,256,256]{3,1,2,0:T(8,128)S(1)} %fusion.19) | data formatting | bytes 12582912 | tf_op jit(solution)/shard_map/vtad,ts->vsad/transpose | solution.py:23
  117.2 0.0 reduce-scatter.2.cloned.1.call-update
  117.2 0.0 copy-done
  117.3 0.2 copy.14
  117.4 0.1 fusion.22
  117.6 83.9 %reduce-scatter.2.cloned.1.call-done = f32[3,128,256]{2,1,0:T(8,128)} async-done(((f32[3,2048,256]{2,1,0:T(8,128)}), f32[3,128,256]{2,1,0:T(8,128)}) %reduce-scatter.2.cloned.1.call-update) | async-done | bytes 393232 | tf_op jit(solution)/shard_map/reduce_scatter | solution.py:26
  201.5 1.2 copy.13
  202.7 1.2 convolution_bitcast_fusion
  204.0 31.1 %all-reduce = (f32[3,3]{0,1:T(4,128)S(1)}, f32[3]{0:T(128)S(1)}) all-reduce(f32[3,3]{0,1:T(4,128)S(1)} %convolution_bitcast_fusion, f32[3]{0:T(128)S(1)} %fusion.22), channel_id=1, replica_groups=mesh['group'=2,'term'=16] {'term'}, use_global_device_ids=true, to_apply=%region_1.2 | all-reduce | flops 12 | bytes 96 | tf_op jit(solution)/shard_map/psum | solution.py:29
  235.1 0.7 gather_fusion.1
  235.7 0.1 rsqrt_multiply_fusion
  235.8 0.7 copy.15
  236.5 1.8 fusion.23
  (3 shorter events, 0.0 us)
Async XLA Ops:
  7.2 51.0 %all-gather.2.cloned.1.call-start = ((), (), s32[]{:S(2)}) async-start(), calls=%async_computation.1 | async-start | bytes 3342336 | tf_op jit(solution)/shard_map/all_gather | solution.py:13
  7.9 193.6 %reduce-scatter.2.cloned.1.call-start = ((), (), s32[]{:S(2)}) async-start(), calls=%async_computation.2 | async-start | bytes 6684672 | tf_op jit(solution)/shard_map/reduce_scatter | solution.py:26
  66.7 17.7 %copy-start.1 = (s32[32]{0:T(128)S(1)}, s32[32]{0:T(128)}, u32[]{:S(2)}) copy-start(s32[32]{0:T(128)} %param.11) | copy-start | bytes 388
  112.7 4.6 %copy-start = (bf16[3,128,256]{2,1,0:T(8,128)(2,1)S(1)}, bf16[3,128,256]{2,1,0:T(8,128)(2,1)}, u32[]{:S(2)}) copy-start(bf16[3,128,256]{2,1,0:T(8,128)(2,1)} %param.6) | copy-start | bytes 589828
Sparse Core Ops, SparseCore 0:
  10.2 47.9 all-gather.1
  117.4 84.0 reduce-scatter.1
where the time goes:
time: 245 us
  waiting for transfers between devices  133 us (54%)
  matrix products  47.1 us (19%)
  blocking collectives  31.1 us (13%)
  local copies, waits for them, and re-layouts  15.9 us (6%)
  between operations  14.1 us (6%)
  other arithmetic  4.08 us (2%)
    reduce_scatter x1, waiting for transfers between devices, local(): lax.psum_scatter(partial_value, 'term', scatter_dimension=1, tiled=True)  83.9 us
    all_gather x1, waiting for transfers between devices, local(): whole = lax.all_gather(vectors, 'term', axis=1, tiled=True)  48.2 us
    psum x1, blocking collectives, local(): proj, norm2 = lax.psum((local_proj, local_norm), 'term')  31.1 us
    dot_general x1, matrix products, local(): jnp.einsum('vtad,ts->vsad', outer, onehot, precision=lax.Precision.HIGHEST)  28.3 us
    dot_general x1, matrix products, local(): jnp.einsum('vtac,tdc->vtad', inner, right_ops, preferred_element_type=jnp...  17.6 us
    gather x1, local copies, waits for them, and re-layouts, local(): picked = jnp.take(blocks, source, axis=1)  8.61 us
  transfers between devices with their start and end apart: 2, of which 2 were waited for; matrix products, arithmetic and copies ran while one was open for 1% of the time, Pallas kernels for 0%

commit v1 on v0

v1 whole, which is shorter than its diff:
```python
import functools

import jax
import jax.numpy as jnp
from jax import lax
from jax.experimental import pallas as pl
from jax.experimental.pallas import tpu as pltpu
from jax.sharding import PartitionSpec as P

CHAIN = 4


def axis_sizes(n):
    chips = n // 2
    inner = 1
    while (inner * 2) ** 2 <= chips:
        inner *= 2
    return chips // inner, inner


def kernel(n, na, nb, nvec, rows, width, sectors, terms,
           coef, src, tgt, vec_in, left_in, right_in,
           sigma, residual, subspace,
           x, left, right, sums, acc, cbuf, crecv, ysend, yrecv, zsend, zrecv, pbuf, precv,
           prev, last,
           load_sem, gz_s, gz_r, gy_s, gy_r, gc_s, gc_r,
           rc_s, rc_r, ry_s, ry_r, rz_s, rz_r, p_s, p_r):
    me = lax.axis_index("term")
    core = lax.rem(me, 2)
    chip = lax.div(me, 2)
    py = lax.rem(chip, nb)
    pz = lax.div(chip, nb)
    half = n // sectors // 2
    factor = sectors / (terms * n)

    def at(z, y, c):
        return (z * nb + y) * 2 + c

    def up(value, step, size):
        return lax.rem(value + step, size)

    def send(source, target, send_sem, recv_sem, device):
        copy = pltpu.make_async_remote_copy(
            src_ref=source, dst_ref=target, send_sem=send_sem, recv_sem=recv_sem,
            device_id={"term": device}, device_id_type=pl.DeviceIdType.MESH)
        return copy

    own = pltpu.make_async_copy(vec_in, x.at[chip // half, lax.rem(chip, half), core], load_sem.at[0])
    own.start()
    loads = [pltpu.make_async_copy(left_in, left, load_sem.at[1]),
             pltpu.make_async_copy(right_in, right, load_sem.at[2])]
    for copy in loads:
        copy.start()

    barrier = pltpu.get_barrier_semaphore()

    def greet(step, carry):
        pl.semaphore_signal(barrier, inc=1, device_id={"term": up(me, step, n)},
                            device_id_type=pl.DeviceIdType.MESH)
        return carry

    lax.fori_loop(1, n, greet, 0)

    ends = tuple(jnp.int32(terms) for _ in range(sectors))

    def link(t, ends):
        target = tgt[t]
        before = jnp.int32(terms)
        for s in range(sectors):
            before = jnp.where(target == s, ends[s], before)
        prev[t] = before
        return tuple(jnp.where(target == s, t, ends[s]) for s in range(sectors))

    ends = lax.fori_loop(0, terms, link, ends)
    for s in range(sectors):
        last[s] = ends[s]
    sums[terms] = jnp.zeros(sums.shape[1:], jnp.float32)

    own.wait()
    pl.semaphore_wait(barrier, n - 1)

    def block(z, y, c):
        k = z * nb + y
        return x.at[lax.div(k, half), lax.rem(k, half), c]

    sent = []

    def start(copy):
        copy.start()
        sent.append(copy)
        return copy

    def to_y_and_core(z, i):
        for o in range(1, nb):
            part = block(z, py, core)
            start(send(part, part, gy_s.at[i, o], gy_r.at[i, o], at(pz, up(py, o, nb), core)))
        part = block(z, py, core)
        start(send(part, part, gc_s.at[i, 0], gc_r.at[i, 0], at(pz, py, 1 - core)))

    def y_arrival(i):
        z = up(pz, na - i, na)
        for o in range(1, nb):
            part = block(z, up(py, nb - o, nb), core)
            send(part, part, gy_s.at[i, o], gy_r.at[i, o], me).wait_recv()
            start(send(part, part, gc_s.at[i, o], gc_r.at[i, o], at(pz, py, 1 - core)))

    for o in range(1, na):
        part = block(pz, py, core)
        start(send(part, part, gz_s.at[o], gz_r.at[o], at(up(pz, o, na), py, core)))
    to_y_and_core(pz, 0)
    for i in range(1, na):
        z = up(pz, na - i, na)
        part = block(z, py, core)
        send(part, part, gz_s.at[i], gz_r.at[i], me).wait_recv()
        to_y_and_core(z, i)
    for i in range(na):
        y_arrival(i)
    for copy in loads:
        copy.wait()
    for i in range(na):
        for o in range(nb):
            part = block(up(pz, na - i, na), up(py, nb - o, nb), 1 - core)
            send(part, part, gc_s.at[i, o], gc_r.at[i, o], me).wait_recv()

    def compute(v, first, stop):
        def body(g, carry):
            ts = [first + g * CHAIN + u for u in range(CHAIN)]
            inner = []
            for t in ts:
                picked = x[src[t], :, :, v].reshape(width, width)
                inner.append(jnp.dot(left[t], picked, preferred_element_type=jnp.float32).astype(jnp.bfloat16))
            outer = [lax.dot_general(a, right[t], (((1,), (1,)), ((), ())), preferred_element_type=jnp.float32)
                     for a, t in zip(inner, ts)]
            for a, t in zip(outer, ts):
                scaled = (a * (coef[t] * factor)).reshape(sums.shape[1:])
                sums[t] = sums[prev[t]] + scaled
            return carry

        lax.fori_loop(0, (stop - first) // CHAIN, body, 0)

    def core_start(v):
        for s in range(sectors):
            end = last[s]
            acc[v, pl.ds(s * half, half)] = sums[end, :, core]
            cbuf[v, pl.ds(s * half, half)] = sums[end, :, 1 - core]
        return start(send(cbuf.at[v], crecv.at[v], rc_s.at[v], rc_r.at[v], at(pz, py, 1 - core)))

    order = list(range(1, na)) + [0]

    def y_start(v, copy):
        copy.wait_recv()
        for i in order:
            z = up(pz, i, na)
            for o in range(1, nb):
                k = z * nb + up(py, o, nb)
                ysend[v, i, o] = (acc[v, k] + crecv[v, k]).astype(jnp.bfloat16)
                start(send(ysend.at[v, i, o], yrecv.at[v, i, o], ry_s.at[v, i, o], ry_r.at[v, i, o],
                           at(pz, up(py, o, nb), core)))

    def z_start(v):
        for i in order:
            z = up(pz, i, na)
            k = z * nb + py
            total = acc[v, k] + crecv[v, k]
            for o in range(1, nb):
                send(ysend.at[v, i, o], yrecv.at[v, i, o], ry_s.at[v, i, o], ry_r.at[v, i, o], me).wait_recv()
                total = total + yrecv[v, i, o].astype(jnp.float32)
            if i == 0:
                sigma[v] = total
            else:
                zsend[v, i] = total.astype(jnp.bfloat16)
                start(send(zsend.at[v, i], zrecv.at[v, i], rz_s.at[v, i], rz_r.at[v, i], at(z, py, core)))

    def finish(v):
        total = sigma[v]
        for i in range(1, na):
            send(zsend.at[v, i], zrecv.at[v, i], rz_s.at[v, i], rz_r.at[v, i], me).wait_recv()
            total = total + zrecv[v, i].astype(jnp.float32)
        sigma[v] = total

    mid = terms // CHAIN // 2 * CHAIN
    waiting = None
    for v in range(nvec):
        compute(v, 0, mid)
        if waiting is not None:
            y_start(v - 1, waiting)
        compute(v, mid, terms)
        waiting = core_start(v)
    y_start(nvec - 1, waiting)

    wide = [x[chip // half, lax.rem(chip, half), core, v].astype(jnp.float32) for v in range(nvec)]

    def lanes(value):
        line = jnp.sum(value, axis=0, keepdims=True)
        return functools.reduce(jnp.add, [line[:, j:j + 128] for j in range(0, width, 128)])

    pbuf[...] = jnp.zeros(pbuf.shape, jnp.float32)
    for v in range(nvec):
        pbuf[pl.ds(nvec * nvec + v, 1)] = lanes(wide[v] * wide[v])
    for v in range(nvec):
        z_start(v)
    for v in range(nvec):
        finish(v)
        for i in range(nvec):
            pbuf[pl.ds(i * nvec + v, 1)] = lanes(wide[i] * sigma[v])

    def small(step):
        return send(pbuf, precv.at[step], p_s.at[step], p_r.at[step], up(me, step, n))

    def put(step, carry):
        small(step).start()
        return carry

    def done(step, carry):
        small(step).wait_send()
        return carry

    lax.fori_loop(1, n, put, 0)
    precv[0] = pbuf[...]

    def arrive(step, carry):
        small(step).wait_recv()
        return carry

    lax.fori_loop(1, n, arrive, 0)

    def add(j, total):
        return total + precv[up(me, n - j, n)]

    total = lax.fori_loop(0, n, add, jnp.zeros(pbuf.shape, jnp.float32))
    whole = jnp.sum(total, axis=1, keepdims=True)
    norm = [whole[nvec * nvec + v:nvec * nvec + v + 1] for v in range(nvec)]
    for v in range(nvec):
        theta = whole[v * nvec + v:v * nvec + v + 1] / norm[v]
        residual[v] = sigma[v] - theta * wide[v]
    row = lax.broadcasted_iota(jnp.int32, (nvec, nvec), 0)
    col = lax.broadcasted_iota(jnp.int32, (nvec, nvec), 1)
    table = jnp.zeros((nvec, nvec), jnp.float32)
    for i in range(nvec):
        for j in range(nvec):
            value = whole[i * nvec + j:i * nvec + j + 1] / jnp.sqrt(norm[i] * norm[j])
            table = jnp.where((row == i) & (col == j), value, table)
    subspace[...] = table
    lax.fori_loop(1, n, done, 0)
    for copy in sent:
        copy.wait_send()


def local(n, vectors, left_ops, right_ops, coefficient, source, target):
    nvec, rows, width = vectors.shape
    terms = left_ops.shape[0]
    sectors = rows * n // width
    na, nb = axis_sizes(n)
    half = n // sectors // 2
    chips = na * nb
    packed = -(-(nvec * nvec + nvec) // 8) * 8
    dma = pltpu.SemaphoreType.DMA
    bf16, f32 = jnp.bfloat16, jnp.float32
    smem = pl.BlockSpec(memory_space=pltpu.SMEM)
    anywhere = pl.BlockSpec(memory_space=pl.ANY)
    vmem = pl.BlockSpec(memory_space=pltpu.VMEM)
    flops = 4 * nvec * terms * width ** 3
    return pl.pallas_call(
        functools.partial(kernel, n, na, nb, nvec, rows, width, sectors, terms),
        out_shape=(jax.ShapeDtypeStruct((nvec, rows, width), f32),
                   jax.ShapeDtypeStruct((nvec, rows, width), f32),
                   jax.ShapeDtypeStruct((nvec, nvec), f32)),
        in_specs=[smem, smem, smem, anywhere, anywhere, anywhere],
        out_specs=(vmem, vmem, vmem),
        scratch_shapes=[
            pltpu.VMEM((sectors, half, 2, nvec, rows, width), bf16),
            pltpu.VMEM((terms, width, width), bf16),
            pltpu.VMEM((terms, width, width), bf16),
            pltpu.VMEM((terms + 1, half, 2, rows, width), f32),
            pltpu.VMEM((nvec, chips, rows, width), f32),
            pltpu.VMEM((nvec, chips, rows, width), f32),
            pltpu.VMEM((nvec, chips, rows, width), f32),
            pltpu.VMEM((nvec, na, nb, rows, width), bf16),
            pltpu.VMEM((nvec, na, nb, rows, width), bf16),
            pltpu.VMEM((nvec, na, rows, width), bf16),
            pltpu.VMEM((nvec, na, rows, width), bf16),
            pltpu.VMEM((packed, 128), f32),
            pltpu.VMEM((n, packed, 128), f32),
            pltpu.SMEM((terms,), jnp.int32),
            pltpu.SMEM((sectors,), jnp.int32),
            dma((3,)),
            dma((na,)), dma((na,)),
            dma((na, nb)), dma((na, nb)),
            dma((na, nb)), dma((na, nb)),
            dma((nvec,)), dma((nvec,)),
            dma((nvec, na, nb)), dma((nvec, na, nb)),
            dma((nvec, na)), dma((nvec, na)),
            dma((n,)), dma((n,)),
        ],
        compiler_params=pltpu.CompilerParams(
            collective_id=0, has_side_effects=True, vmem_limit_bytes=52 * 2 ** 20),
        cost_estimate=pl.CostEstimate(
            flops=flops, bytes_accessed=4 * terms * width ** 2, transcendentals=0),
    )(coefficient, source, target, vectors, left_ops, right_ops)


def solution(mesh):
    n = mesh.shape["term"]
    in_specs = (
        P("group", "term", None),
        P(("group", "term"), None, None),
        P(("group", "term"), None, None),
        P(("group", "term")),
        P(("group", "term")),
        P(("group", "term")),
    )
    out_specs = (P("group", "term", None), P("group", "term", None), P("group", None))
    return jax.shard_map(functools.partial(local, n), mesh=mesh, in_specs=in_specs,
                         out_specs=out_specs, check_vma=False)
```

time: 245 us -> 78.9 us (0.32)
  waiting for transfers between devices: 133 us -> 0 us
  Pallas kernels: 0 us -> 73.1 us
  matrix products: 47.1 us -> 0 us
  blocking collectives: 31.1 us -> 0 us
  between operations: 14.1 us -> 0.65 us
  local copies, waits for them, and re-layouts: 15.9 us -> 4.96 us
  other arithmetic: 4.08 us -> 0 us
    reduce_scatter x1 -> x0, waiting for transfers between devices: 83.9 us -> none  [local(): lax.psum_scatter(partial_value, 'term', scatter_dimension=1, tiled=True)]
    pallas_call x0 -> x1, Pallas kernels: none -> 73.1 us  [local(): pl.pallas_call(functools.partial(kernel, n, na, nb, nvec, rows, width, se...]
    all_gather x1 -> x0, waiting for transfers between devices: 48.2 us -> none  [local(): whole = lax.all_gather(vectors, 'term', axis=1, tiled=True)]
    dot_general x3 -> x0, matrix products: 47.1 us -> none  [the longest x1 28.3 us: local(): jnp.einsum('vtad,ts->vsad', outer, onehot, precision=lax.Precision.HIGHEST)]
    psum x1 -> x0, blocking collectives: 31.1 us -> none  [local(): proj, norm2 = lax.psum((local_proj, local_norm), 'term')]
    gather x2 -> x0, local copies, waits for them, and re-layouts: 9.26 us -> none  [the longest x1 8.61 us: local(): picked = jnp.take(blocks, source, axis=1)]
    transpose x1 -> x0, local copies, waits for them, and re-layouts: 4.55 us -> none  [local(): jnp.einsum('vtad,ts->vsad', outer, onehot, precision=lax.Precision.HIGHEST)]
    unnamed x6 -> x11, local copies, waits for them, and re-layouts: 0.86 us -> 4.96 us
  transfers between devices with their start and end apart: 2 -> 0, of which waited for: 2 -> 0; matrix products, arithmetic and copies ran while one was open for 1% -> 0% of each run, Pallas kernels for 0% -> 0%
where the time goes in v1:
time: 78.9 us; the launch traced here: 78.7 us
  Pallas kernels  73.1 us (93%)
  local copies, waits for them, and re-layouts  4.96 us (6%)
    pallas_call x1, Pallas kernels, local(): pl.pallas_call(functools.partial(kernel, n, na, nb, nvec, rows, width, se...  73.1 us
    unnamed x11, local copies, waits for them, and re-layouts  4.96 us

profile of v1, /device:TPU:0, one launch (start us, length us, event | category | flops | bytes accessed | tf_op | source)
XLA Modules:
  0.0 78.7 jit_solution(9661836636746089469)
XLA Ops:
  0.6 0.0 copy-start
  0.6 0.9 %copy-done = bf16[3,128,256]{2,1,0:T(8,128)(2,1)S(1)} copy-done((bf16[3,128,256]{2,1,0:T(8,128)(2,1)S(1)}, bf16[3,128,256]{2,1,0:T(8,128)(2,1)}, u32[]{:S(2)}) %copy-start) | copy-done | bytes 196632
  1.6 0.0 copy-start.1
  1.6 0.7 copy-done.1
  2.2 0.0 copy-start.2
  2.2 0.7 copy-done.2
  2.9 0.0 copy-start.3
  2.9 0.7 copy-done.3
  3.5 73.1 %shard_map.85 = (f32[3,128,256]{2,1,0:T(8,128)S(1)}, f32[3,128,256]{2,1,0:T(8,128)S(1)}, f32[3,3]{1,0:T(4,128)S(1)}) custom-call(f32[32]{0:T(128)S(1)} %copy-done.1, s32[32]{0:T(128)S(1)} %copy-done.2, s32[32]{0:T(128)S(1)} %copy-done.3, bf16[3,128,256]{2,1,0:T(8,128)(2,1)S(1)} %copy-done, bf16[32,256,256]{2,1,0:T(8,128)(2,1)} %left_in.1, ...), custom_call_target="tpu_custom_call" | custom-call | flops 6442450944 | bytes 8388608 | tf_op jit(solution)/shard_map/pallas_call | solution.py:263
  76.7 0.7 copy.12
  77.4 0.7 copy.13
  78.2 0.6 copy.14
Async XLA Ops:
  0.6 0.9 %copy-start = (bf16[3,128,256]{2,1,0:T(8,128)(2,1)S(1)}, bf16[3,128,256]{2,1,0:T(8,128)(2,1)}, u32[]{:S(2)}) copy-start(bf16[3,128,256]{2,1,0:T(8,128)(2,1)} %vec_in.1) | copy-start | bytes 589828
  1.6 0.7 copy-start.1
  2.2 0.7 copy-start.2
  2.9 0.7 copy-start.3

commit v2 on v1

--- a/solution.py
+++ b/solution.py
@@ -8,6 +8,11 @@
 from jax.sharding import PartitionSpec as P
 
 CHAIN = 4
+ORDER = (
+    "O0", "O1", "Z0", "O2", "Y0", "Z1", "A0", "C0", "Y1",
+    "Z2", "D0", "S0", "A1", "C1", "Y2", "P0", "D1", "S1",
+    "A2", "P1", "C2", "Q0", "D2", "S2", "P2", "Q1", "Q2",
+)
 
 
 def axis_sizes(n):
@@ -19,10 +24,10 @@
 
 
 def kernel(n, na, nb, nvec, rows, width, sectors, terms,
-           coef, src, tgt, vec_in, left_in, right_in,
+           coef_in, src_in, tgt_in, vec_in, left_in, right_in,
            sigma, residual, subspace,
            x, left, right, sums, acc, cbuf, crecv, ysend, yrecv, zsend, zrecv, pbuf, precv,
-           prev, last,
+           coef, src, tgt, prev, last,
            load_sem, gz_s, gz_r, gy_s, gy_r, gc_s, gc_r,
            rc_s, rc_r, ry_s, ry_r, rz_s, rz_r, p_s, p_r):
     me = lax.axis_index("term")
@@ -45,10 +50,16 @@
             device_id={"term": device}, device_id_type=pl.DeviceIdType.MESH)
         return copy
 
-    own = pltpu.make_async_copy(vec_in, x.at[chip // half, lax.rem(chip, half), core], load_sem.at[0])
-    own.start()
-    loads = [pltpu.make_async_copy(left_in, left, load_sem.at[1]),
-             pltpu.make_async_copy(right_in, right, load_sem.at[2])]
+    mine = [x[v].at[chip // half, lax.rem(chip, half), core] for v in range(nvec)]
+    own = [pltpu.make_async_copy(vec_in.at[v], mine[v], load_sem.at[5 + v]) for v in range(nvec)]
+    for copy in own:
+        copy.start()
+    scalars = [pltpu.make_async_copy(src_ref=a, dst_ref=b, sem=load_sem.at[2 + j])
+               for j, (a, b) in enumerate(((coef_in, coef), (src_in, src), (tgt_in, tgt)))]
+    for copy in scalars:
+        copy.start()
+    loads = [pltpu.make_async_copy(left_in, left, load_sem.at[0]),
+             pltpu.make_async_copy(right_in, right, load_sem.at[1])]
     for copy in loads:
         copy.start()
 
@@ -60,6 +71,9 @@
         return carry
 
     lax.fori_loop(1, n, greet, 0)
+
+    for copy in scalars:
+        copy.wait()
 
     ends = tuple(jnp.int32(terms) for _ in range(sectors))
 
@@ -76,12 +90,13 @@
         last[s] = ends[s]
     sums[terms] = jnp.zeros(sums.shape[1:], jnp.float32)
 
-    own.wait()
+    for copy in own:
+        copy.wait()
     pl.semaphore_wait(barrier, n - 1)
 
-    def block(z, y, c):
+    def block(v, z, y, c):
         k = z * nb + y
-        return x.at[lax.div(k, half), lax.rem(k, half), c]
+        return x[v].at[lax.div(k, half), lax.rem(k, half), c]
 
     sent = []
 
@@ -90,44 +105,45 @@
         sent.append(copy)
         return copy
 
-    def to_y_and_core(z, i):
+    def own_start(v):
+        part = block(v, pz, py, core)
+        for o in range(1, na):
+            start(send(part, part, gz_s.at[v, o], gz_r.at[v, o], at(up(pz, o, na), py, core)))
+        to_y_and_core(v, pz, 0)
+
+    def to_y_and_core(v, z, i):
+        part = block(v, z, py, core)
         for o in range(1, nb):
-            part = block(z, py, core)
-            start(send(part, part, gy_s.at[i, o], gy_r.at[i, o], at(pz, up(py, o, nb), core)))
-        part = block(z, py, core)
-        start(send(part, part, gc_s.at[i, 0], gc_r.at[i, 0], at(pz, py, 1 - core)))
-
-    def y_arrival(i):
-        z = up(pz, na - i, na)
-        for o in range(1, nb):
-            part = block(z, up(py, nb - o, nb), core)
-            send(part, part, gy_s.at[i, o], gy_r.at[i, o], me).wait_recv()
-            start(send(part, part, gc_s.at[i, o], gc_r.at[i, o], at(pz, py, 1 - core)))
-
-    for o in range(1, na):
-        part = block(pz, py, core)
-        start(send(part, part, gz_s.at[o], gz_r.at[o], at(up(pz, o, na), py, core)))
-    to_y_and_core(pz, 0)
-    for i in range(1, na):
-        z = up(pz, na - i, na)
-        part = block(z, py, core)
-        send(part, part, gz_s.at[i], gz_r.at[i], me).wait_recv()
-        to_y_and_core(z, i)
-    for i in range(na):
-        y_arrival(i)
-    for copy in loads:
-        copy.wait()
-    for i in range(na):
-        for o in range(nb):
-            part = block(up(pz, na - i, na), up(py, nb - o, nb), 1 - core)
-            send(part, part, gc_s.at[i, o], gc_r.at[i, o], me).wait_recv()
+            start(send(part, part, gy_s.at[v, i, o], gy_r.at[v, i, o], at(pz, up(py, o, nb), core)))
+        start(send(part, part, gc_s.at[v, i, 0], gc_r.at[v, i, 0], at(pz, py, 1 - core)))
+
+    def z_arrivals(v):
+        for i in range(1, na):
+            z = up(pz, na - i, na)
+            part = block(v, z, py, core)
+            send(part, part, gz_s.at[v, i], gz_r.at[v, i], me).wait_recv()
+            to_y_and_core(v, z, i)
+
+    def y_arrivals(v):
+        for i in range(na):
+            z = up(pz, na - i, na)
+            for o in range(1, nb):
+                part = block(v, z, up(py, nb - o, nb), core)
+                send(part, part, gy_s.at[v, i, o], gy_r.at[v, i, o], me).wait_recv()
+                start(send(part, part, gc_s.at[v, i, o], gc_r.at[v, i, o], at(pz, py, 1 - core)))
+
+    def core_arrivals(v):
+        for i in range(na):
+            for o in range(nb):
+                part = block(v, up(pz, na - i, na), up(py, nb - o, nb), 1 - core)
+                send(part, part, gc_s.at[v, i, o], gc_r.at[v, i, o], me).wait_recv()
 
     def compute(v, first, stop):
         def body(g, carry):
             ts = [first + g * CHAIN + u for u in range(CHAIN)]
             inner = []
             for t in ts:
-                picked = x[src[t], :, :, v].reshape(width, width)
+                picked = x[v][src[t]].reshape(width, width)
                 inner.append(jnp.dot(left[t], picked, preferred_element_type=jnp.float32).astype(jnp.bfloat16))
             outer = [lax.dot_general(a, right[t], (((1,), (1,)), ((), ())), preferred_element_type=jnp.float32)
                      for a, t in zip(inner, ts)]
@@ -143,12 +159,12 @@
             end = last[s]
             acc[v, pl.ds(s * half, half)] = sums[end, :, core]
             cbuf[v, pl.ds(s * half, half)] = sums[end, :, 1 - core]
-        return start(send(cbuf.at[v], crecv.at[v], rc_s.at[v], rc_r.at[v], at(pz, py, 1 - core)))
+        start(send(cbuf.at[v], crecv.at[v], rc_s.at[v], rc_r.at[v], at(pz, py, 1 - core)))
 
     order = list(range(1, na)) + [0]
 
-    def y_start(v, copy):
-        copy.wait_recv()
+    def y_start(v):
+        send(cbuf.at[v], crecv.at[v], rc_s.at[v], rc_r.at[v], me).wait_recv()
         for i in order:
             z = up(pz, i, na)
             for o in range(1, nb):
@@ -179,16 +195,21 @@
         sigma[v] = total
 
     mid = terms // CHAIN // 2 * CHAIN
-    waiting = None
-    for v in range(nvec):
-        compute(v, 0, mid)
-        if waiting is not None:
-            y_start(v - 1, waiting)
-        compute(v, mid, terms)
-        waiting = core_start(v)
-    y_start(nvec - 1, waiting)
-
-    wide = [x[chip // half, lax.rem(chip, half), core, v].astype(jnp.float32) for v in range(nvec)]
+    steps = {"O": own_start, "Z": z_arrivals, "Y": y_arrivals, "A": core_arrivals, "S": core_start,
+             "P": y_start, "Q": z_start, "C": lambda v: compute(v, 0, mid), "D": lambda v: compute(v, mid, terms)}
+    if nvec == 3:
+        plan = ORDER
+    else:
+        plan = [step + str(v) for v in range(nvec) for step in "OZYACDSPQ"]
+    plan = list(plan)
+    first = [step[0] for step in plan].index("C")
+    for j, step in enumerate(plan):
+        if j == first:
+            for copy in loads:
+                copy.wait()
+        steps[step[0]](int(step[1:]))
+
+    wide = [mine[v][...].astype(jnp.float32) for v in range(nvec)]
 
     def lanes(value):
         line = jnp.sum(value, axis=0, keepdims=True)
@@ -197,8 +218,6 @@
     pbuf[...] = jnp.zeros(pbuf.shape, jnp.float32)
     for v in range(nvec):
         pbuf[pl.ds(nvec * nvec + v, 1)] = lanes(wide[v] * wide[v])
-    for v in range(nvec):
-        z_start(v)
     for v in range(nvec):
         finish(v)
         for i in range(nvec):
@@ -256,8 +275,7 @@
     packed = -(-(nvec * nvec + nvec) // 8) * 8
     dma = pltpu.SemaphoreType.DMA
     bf16, f32 = jnp.bfloat16, jnp.float32
-    smem = pl.BlockSpec(memory_space=pltpu.SMEM)
-    anywhere = pl.BlockSpec(memory_space=pl.ANY)
+    anywhere = pl.BlockSpec(memory_space=pltpu.HBM)
     vmem = pl.BlockSpec(memory_space=pltpu.VMEM)
     flops = 4 * nvec * terms * width ** 3
     return pl.pallas_call(
@@ -265,10 +283,10 @@
         out_shape=(jax.ShapeDtypeStruct((nvec, rows, width), f32),
                    jax.ShapeDtypeStruct((nvec, rows, width), f32),
                    jax.ShapeDtypeStruct((nvec, nvec), f32)),
-        in_specs=[smem, smem, smem, anywhere, anywhere, anywhere],
+        in_specs=[anywhere] * 6,
         out_specs=(vmem, vmem, vmem),
         scratch_shapes=[
-            pltpu.VMEM((sectors, half, 2, nvec, rows, width), bf16),
+            tuple(pltpu.VMEM((sectors, half, 2, rows, width), bf16) for _ in range(nvec)),
             pltpu.VMEM((terms, width, width), bf16),
             pltpu.VMEM((terms, width, width), bf16),
             pltpu.VMEM((terms + 1, half, 2, rows, width), f32),
@@ -281,12 +299,15 @@
             pltpu.VMEM((nvec, na, rows, width), bf16),
             pltpu.VMEM((packed, 128), f32),
             pltpu.VMEM((n, packed, 128), f32),
+            pltpu.SMEM((terms,), f32),
+            pltpu.SMEM((terms,), jnp.int32),
+            pltpu.SMEM((terms,), jnp.int32),
             pltpu.SMEM((terms,), jnp.int32),
             pltpu.SMEM((sectors,), jnp.int32),
-            dma((3,)),
-            dma((na,)), dma((na,)),
-            dma((na, nb)), dma((na, nb)),
-            dma((na, nb)), dma((na, nb)),
+            dma((5 + nvec,)),
+            dma((nvec, na)), dma((nvec, na)),
+            dma((nvec, na, nb)), dma((nvec, na, nb)),
+            dma((nvec, na, nb)), dma((nvec, na, nb)),
             dma((nvec,)), dma((nvec,)),
             dma((nvec, na, nb)), dma((nvec, na, nb)),
             dma((nvec, na)), dma((nvec, na)),

time: 78.9 us -> 69.2 us (0.88)
  Pallas kernels: 73.1 us -> 63.4 us
    pallas_call x1, Pallas kernels: 73.1 us -> 63.4 us  [local(): pl.pallas_call(functools.partial(kernel, n, na, nb, nvec, rows, width, se...]
where the time goes in v2:
time: 69.2 us; the launch traced here: 69 us
  Pallas kernels  63.4 us (92%)
  local copies, waits for them, and re-layouts  4.96 us (7%)
    pallas_call x1, Pallas kernels, local(): pl.pallas_call(functools.partial(kernel, n, na, nb, nvec, rows, width, se...  63.4 us
    unnamed x11, local copies, waits for them, and re-layouts  4.96 us

profile of v2, /device:TPU:0, one launch (start us, length us, event | category | flops | bytes accessed | tf_op | source)
XLA Modules:
  0.0 69.0 jit_solution(16033449735797793747)
XLA Ops:
  0.6 0.0 copy-start
  0.6 0.9 %copy-done = bf16[3,128,256]{2,1,0:T(8,128)(2,1)S(1)} copy-done((bf16[3,128,256]{2,1,0:T(8,128)(2,1)S(1)}, bf16[3,128,256]{2,1,0:T(8,128)(2,1)}, u32[]{:S(2)}) %copy-start) | copy-done | bytes 196632
  1.6 0.0 copy-start.1
  1.6 0.7 copy-done.1
  2.2 0.0 copy-start.2
  2.2 0.7 copy-done.2
  2.9 0.0 copy-start.3
  2.9 0.7 copy-done.3
  3.5 63.4 %shard_map.85 = (f32[3,128,256]{2,1,0:T(8,128)S(1)}, f32[3,128,256]{2,1,0:T(8,128)S(1)}, f32[3,3]{1,0:T(4,128)S(1)}) custom-call(f32[32]{0:T(128)S(1)} %copy-done.1, s32[32]{0:T(128)S(1)} %copy-done.2, s32[32]{0:T(128)S(1)} %copy-done.3, bf16[3,128,256]{2,1,0:T(8,128)(2,1)S(1)} %copy-done, bf16[32,256,256]{2,1,0:T(8,128)(2,1)} %left_in.1, ...), custom_call_target="tpu_custom_call" | custom-call | flops 6442450944 | bytes 8388608 | tf_op jit(solution)/shard_map/pallas_call | solution.py:281
  67.0 0.7 %copy.12 = f32[3,128,256]{2,1,0:T(8,128)} copy(f32[3,128,256]{2,1,0:T(8,128)S(1)} %get-tuple-element.6) | data formatting | bytes 786432
  67.7 0.7 %copy.13 = f32[3,128,256]{2,1,0:T(8,128)} copy(f32[3,128,256]{2,1,0:T(8,128)S(1)} %get-tuple-element.7) | data formatting | bytes 786432
  68.4 0.6 copy.14
Async XLA Ops:
  0.6 0.9 %copy-start = (bf16[3,128,256]{2,1,0:T(8,128)(2,1)S(1)}, bf16[3,128,256]{2,1,0:T(8,128)(2,1)}, u32[]{:S(2)}) copy-start(bf16[3,128,256]{2,1,0:T(8,128)(2,1)} %vec_in.1) | copy-start | bytes 589828
  1.6 0.7 copy-start.1
  2.2 0.7 copy-start.2
  2.9 0.7 copy-start.3
